TPU v7x, 32 devices: a whole 2x2x4 slice. The times are simulated.
32 devices in a mesh: groups: 2 (over y), renv: 16 (over z, x, core).
Axes of the slice: x: 2, y: 2, z: 4, core: 2. Of those that a mesh axis runs over, the one named last changes fastest.
Arguments:
- psi: float32 [256, 16384], P(('groups', 'renv')), parts along dimension 0, may hold values from -18 to 18, as said below
- left_env: float32 [128, 16384], P('groups'), parts along dimension 0, may hold values from -1 to 1.5
- right_env: float32 [512, 16384], P(('groups', 'renv')), parts along dimension 0, may hold values from -1 to 1.5
- send_block: int32 [512, 1], P(('groups', 'renv')), parts along dimension 0, may hold values from 0 to 7
- send_left: int32 [512, 1, 2], P(('groups', 'renv')), parts along dimension 0, may hold values from 0 to 63
- send_live: int32 [512, 1, 2], P(('groups', 'renv')), parts along dimension 0, may hold values from 0 to 1, as said below
- recv_right: int32 [512, 1, 2], P(('groups', 'renv')), parts along dimension 0, may hold values from 0 to 15
- recv_out: int32 [512, 1, 2], P(('groups', 'renv')), parts along dimension 0, may hold values from 0 to 7
- loc_block: int32 [1024], P(('groups', 'renv')), parts along dimension 0, may hold values from 0 to 7
- loc_left: int32 [1024], P(('groups', 'renv')), parts along dimension 0, may hold values from 0 to 63
- loc_right: int32 [1024], P(('groups', 'renv')), parts along dimension 0, may hold values from 0 to 15
Outputs:
- hpsi: float32 [256, 16384], P(('groups', 'renv')), parts along dimension 0
- residual: float32 [256, 16384], P(('groups', 'renv')), parts along dimension 0
There are 2 independent parts, one for each index of `groups`. A program takes and returns all parts, laid end to end along the dimension named above; each array names one. Nothing has to cross between parts.
Inputs may be any that keep to these rules, and one draw needn't show every extreme that they name: psi blocks of owner-ordered index i have entries of size growing with i. `send_live`: in every draw some receiver has every term live from every sender.
All inputs are finite; a program needn't handle non-finite values.
Results may differ from a plain program's by a relative error of at most 0.0003.
Values sent between devices are 32-bit elements; how exact they have to be, the bound alone decides.
No kernel may reach another device: no remote copies, remote signals or barrier semaphores. Data moves between devices by JAX's collectives and lax.ppermute only.
A program may use at most 128 MiB of HBM per device.

v0:
```python
import math

import jax
import jax.numpy as jnp
from jax import lax
from jax.experimental import pallas as pl
from jax.experimental.pallas import tpu as pltpu
from jax.sharding import PartitionSpec as P

F32 = jnp.float32
BF16 = jnp.bfloat16
SUB = 8
VMEM = pl.BlockSpec(memory_space=pltpu.VMEM)
SMEM = pl.BlockSpec(memory_space=pltpu.SMEM)
HBM = pl.BlockSpec(memory_space=pltpu.HBM)
MIB = 2**20
LIGHT = pl.CostEstimate(flops=10**6, bytes_accessed=2**16, transcendentals=0)


def as_rows(blocks, sector):
    count = blocks.shape[0]
    split = blocks.reshape(count // SUB, SUB, sector, sector)
    return split.transpose(0, 2, 1, 3).reshape(count * sector, sector)


def from_rows(rows, count):
    sector = rows.shape[1]
    split = rows.reshape(count // SUB, sector, SUB, sector)
    return split.transpose(0, 2, 1, 3).reshape(count, sector * sector)


def pick(ref, block):
    sector = ref.shape[1]
    start = (block // SUB) * (SUB * sector) + block % SUB
    return ref[pl.ds(start, sector, stride=SUB), :]


def halves(mat):
    high = mat.astype(BF16)
    low = (mat - high.astype(F32)).astype(BF16)
    return jnp.concatenate([high, low], axis=1)


def doubled(mat):
    both = halves(mat)
    return jnp.concatenate([both, both], axis=0)


def product(left, right):
    sector = right.shape[1] // 2
    wide = jnp.dot(left, right, preferred_element_type=F32)
    return wide[:, :sector] + wide[:, sector:]


def stacked(mat):
    high = mat.astype(BF16)
    low = (mat - high.astype(F32)).astype(BF16)
    rows = [jnp.concatenate([part, part], axis=1) for part in (high, low)]
    return jnp.concatenate(rows, axis=0)


def product_t(left, right):
    sector = right.shape[0] // 2
    wide = lax.dot_general(left, right, (((1,), (1,)), ((), ())), preferred_element_type=F32)
    return wide[:, :sector] + wide[:, sector:]


def twice(part):
    return jnp.concatenate([part, part], axis=0)


def roomy(mib):
    return pltpu.CompilerParams(vmem_limit_bytes=mib * MIB)


def gather_kernel(block_ref, psi_rows, out_hbm, stage, sems):
    puts = []
    for i in range(stage.shape[0]):
        stage[i] = pick(psi_rows, block_ref[i])
        put = pltpu.make_async_copy(stage.at[i], out_hbm.at[i], sems.at[i])
        put.start()
        puts.append(put)
    for put in puts:
        put.wait()


def index_kernel(sent_hbm, left_ref, live_ref, meta_ref):
    slots, terms, peers = left_ref.shape
    lane = lax.broadcasted_iota(jnp.int32, meta_ref.shape, 1)
    values = jnp.zeros(meta_ref.shape, jnp.int32)
    for i in range(peers * slots):
        for g in range(terms):
            at = i * 2 * terms + g
            values = jnp.where(lane == at, left_ref[i % slots, g, i // slots], values)
            values = jnp.where(lane == at + terms, live_ref[i % slots, g, i // slots], values)
    meta_ref[...] = values


def turn_kernel(sent_hbm, rindex_ref, out_index_ref, psi_rows, right_rows, turned_ref, rights_ref, psis_ref, stacks_ref):
    slots, terms, _ = rindex_ref.shape

    def split_right(i, carry):
        rights_ref[i] = halves(pick(right_rows, i))
        return carry

    lax.fori_loop(0, rights_ref.shape[0], split_right, 0, unroll=4)

    def split_psi(i, carry):
        mat = pick(psi_rows, i)
        psis_ref[i] = halves(mat)
        stacks_ref[i] = stacked(mat)
        return carry

    lax.fori_loop(0, psis_ref.shape[0], split_psi, 0, unroll=4)

    def turn(i, carry):
        inner = []
        for g in range(terms):
            right = rights_ref[rindex_ref[i % slots, g, i // slots]]
            inner.append(halves(product_t(right, stacks_ref[out_index_ref[i % slots, g, i // slots]])))
        turned_ref[i] = jnp.concatenate(inner, axis=1)
        return carry

    lax.fori_loop(0, turned_ref.shape[0], turn, 0, unroll=4)


def local_kernel(block_ref, left_ref, right_ref, psi_rows, left_rows, psis_ref, rights_ref, near_ref, sums_ref, moved_ref):
    near_ref[...] = jnp.zeros_like(near_ref)

    def left_step(k, carry):
        moved = product(halves(pick(left_rows, left_ref[k])), twice(psis_ref[block_ref[k]]))
        moved_ref[k] = halves(moved)
        return carry

    lax.fori_loop(0, block_ref.shape[0], left_step, 0, unroll=8)

    def right_step(k, carry):
        near_ref[block_ref[k]] += product(moved_ref[k], twice(rights_ref[right_ref[k]]))
        return carry

    lax.fori_loop(0, block_ref.shape[0], right_step, 0, unroll=8)
    corr = jnp.zeros((1, sums_ref.shape[1]), F32)
    norm = jnp.zeros((1, sums_ref.shape[1]), F32)
    for b in range(near_ref.shape[0]):
        mat = pick(psi_rows, b)
        corr += jnp.sum(mat * near_ref[b], axis=0, keepdims=True)
        norm += jnp.sum(mat * mat, axis=0, keepdims=True)
    row = lax.broadcasted_iota(jnp.int32, sums_ref.shape, 0)
    sums_ref[...] = jnp.where(row == 0, corr, jnp.where(row == 1, norm, 0.0))


def adjoint_kernel(slots, terms, me_ref, meta_ref, left_rows, turned_ref, adjoint_ref, lefts_ref):
    sector = left_rows.shape[1]

    def sender(i, carry):
        weights = []
        row = lax.bitwise_xor(i // slots, me_ref[0])
        base = (me_ref[0] * slots + i % slots) * 2 * terms
        for g in range(terms):
            live = meta_ref[row, base + terms + g].astype(F32)
            left = halves(pick(left_rows, meta_ref[row, base + g]) * live)
            lefts_ref[i, g * sector : (g + 1) * sector] = left
            weights.append(twice(left))
        adjoint_ref[i] = product(turned_ref[i], jnp.concatenate(weights, axis=0)).T
        return carry

    lax.fori_loop(0, adjoint_ref.shape[0], sender, 0, unroll=4)


def overlap_kernel(came_ref, adjoint_ref, near_sums_ref, out_ref):
    def block(i, total):
        return total + jnp.sum((came_ref[i] * adjoint_ref[i]).reshape(-1, SUB, came_ref.shape[2]), axis=0)

    total = lax.fori_loop(0, came_ref.shape[0], block, jnp.zeros(out_ref.shape[1:], F32), unroll=4)
    corr = jnp.sum(total, axis=0, keepdims=True)
    row = lax.broadcasted_iota(jnp.int32, total.shape, 0)
    mine = near_sums_ref[...] + jnp.where(row == 0, corr, 0.0)
    for i in range(out_ref.shape[0]):
        out_ref[i] = mine


def remote_kernel(rindex_ref, out_index_ref, came_ref, near_ref, lefts_ref, rights_ref, hpsi_rows, hpsi_hbm, acc, moved_ref, sem):
    count, sector, _ = came_ref.shape
    slots, terms, _ = rindex_ref.shape
    acc[...] = near_ref[...]

    def left_step(i, carry):
        moved_ref[i] = halves(product(lefts_ref[i], doubled(came_ref[i])))
        return carry

    lax.fori_loop(0, count, left_step, 0, unroll=4)

    def right_step(i, carry):
        for g in range(terms):
            right = rights_ref[rindex_ref[i % slots, g, i // slots]]
            acc[out_index_ref[i % slots, g, i // slots]] += product(moved_ref[i, g * sector : (g + 1) * sector], twice(right))
        return carry

    lax.fori_loop(0, count, right_step, 0, unroll=4)
    for b in range(acc.shape[0]):
        start = (b // SUB) * (SUB * sector) + b % SUB
        hpsi_rows[pl.ds(start, sector, stride=SUB), :] = acc[b]
    put = pltpu.make_async_copy(hpsi_rows, hpsi_hbm, sem)
    put.start()
    put.wait()


def residual_kernel(sums_ref, hpsi_rows, psi_rows, out_ref):
    total = jnp.sum(sums_ref[...], axis=0)
    whole = jnp.sum(total, axis=1, keepdims=True)
    theta = whole[0:1] / (whole[1:2] + 1e-06)
    out_ref[...] = hpsi_rows[...] - theta * psi_rows[...]


def shards(
    psi,
    left_env,
    right_env,
    send_block,
    send_left,
    send_live,
    recv_right,
    recv_out,
    loc_block,
    loc_left,
    loc_right,
):
    peers = lax.axis_size("renv")
    owned = psi.shape[0]
    sector = math.isqrt(psi.shape[1])
    slots = send_block.shape[1]
    terms = send_left.shape[2]
    count = peers * slots
    rights = right_env.shape[0]
    psi_rows = as_rows(psi, sector)
    left_rows = as_rows(left_env, sector)
    right_rows = as_rows(right_env, sector)
    me = lax.axis_index("renv").astype(jnp.int32).reshape(1)
    by_slot = [index.transpose(1, 2, 0) for index in (send_left, send_live, recv_right, recv_out)]
    blocks = jax.ShapeDtypeStruct((count, sector, sector), F32)
    rows = jax.ShapeDtypeStruct((owned * sector, sector), F32)
    mats = jax.ShapeDtypeStruct((owned, sector, sector), F32)
    tile = jax.ShapeDtypeStruct((SUB, sector), F32)

    sent = pl.pallas_call(
        gather_kernel,
        out_shape=blocks,
        in_specs=[SMEM, VMEM],
        out_specs=HBM,
        scratch_shapes=[pltpu.VMEM(blocks.shape, F32), pltpu.SemaphoreType.DMA((count,))],
        compiler_params=roomy(56),
        name="gather_blocks",
    )(send_block.reshape(-1), psi_rows)
    came = lax.all_to_all(sent.reshape(peers, slots, sector, sector), "renv", split_axis=0, concat_axis=0, tiled=True)
    came = came.reshape(count, sector, sector)

    lanes = -(-count * 2 * terms // 128) * 128
    meta = pl.pallas_call(
        index_kernel,
        out_shape=jax.ShapeDtypeStruct((1, lanes), jnp.int32),
        in_specs=[HBM] + [SMEM] * 2,
        out_specs=VMEM,
        compiler_params=roomy(56),
        cost_estimate=LIGHT,
        name="index_rows",
    )(sent, *by_slot[:2])
    step = 1
    while step < peers:
        meta = jnp.concatenate([meta, lax.ppermute(meta, "renv", [(s, s ^ step) for s in range(peers)])], axis=0)
        step *= 2

    turned, right_parts, psi_parts = pl.pallas_call(
        turn_kernel,
        out_shape=(
            jax.ShapeDtypeStruct((count, sector, terms * 2 * sector), BF16),
            jax.ShapeDtypeStruct((rights, sector, 2 * sector), BF16),
            jax.ShapeDtypeStruct((owned, sector, 2 * sector), BF16),
        ),
        in_specs=[HBM] + [SMEM] * 2 + [VMEM] * 2,
        out_specs=(VMEM,) * 3,
        scratch_shapes=[pltpu.VMEM((owned, 2 * sector, 2 * sector), BF16)],
        compiler_params=roomy(56),
        cost_estimate=LIGHT,
        name="turn",
    )(sent, *by_slot[2:], psi_rows, right_rows)

    near, near_sums = pl.pallas_call(
        local_kernel,
        out_shape=(mats, tile),
        in_specs=[SMEM] * 3 + [VMEM] * 4,
        out_specs=(VMEM,) * 2,
        scratch_shapes=[pltpu.VMEM((loc_block.shape[0], sector, 2 * sector), BF16)],
        compiler_params=roomy(56),
        cost_estimate=LIGHT,
        name="local_terms",
    )(loc_block, loc_left, loc_right, psi_rows, left_rows, psi_parts, right_parts)

    adjoint, left_parts = pl.pallas_call(
        lambda *refs: adjoint_kernel(slots, terms, *refs),
        out_shape=(blocks, jax.ShapeDtypeStruct((count, terms * sector, 2 * sector), BF16)),
        in_specs=[SMEM] * 2 + [VMEM] * 2,
        out_specs=(VMEM,) * 2,
        compiler_params=roomy(48),
        cost_estimate=LIGHT,
        name="adjoint_blocks",
    )(me, meta, left_rows, turned)

    sums = pl.pallas_call(
        overlap_kernel,
        out_shape=jax.ShapeDtypeStruct((peers, SUB, sector), F32),
        in_specs=[VMEM] * 3,
        out_specs=VMEM,
        compiler_params=roomy(24),
        name="overlap",
    )(came, adjoint, near_sums)
    sums = lax.all_to_all(sums, "renv", split_axis=0, concat_axis=0, tiled=True)

    hpsi_rows, hpsi = pl.pallas_call(
        remote_kernel,
        out_shape=(rows, rows),
        in_specs=[SMEM] * 2 + [VMEM] * 4,
        out_specs=(VMEM, HBM),
        scratch_shapes=[
            pltpu.VMEM(mats.shape, F32),
            pltpu.VMEM((count, terms * sector, 2 * sector), BF16),
            pltpu.SemaphoreType.DMA,
        ],
        compiler_params=roomy(48),
        cost_estimate=pl.CostEstimate(flops=4 * 10**9, bytes_accessed=6 * MIB, transcendentals=0),
        name="remote_terms",
    )(*by_slot[2:], came, near, left_parts, right_parts)

    residual_rows = pl.pallas_call(
        residual_kernel,
        out_shape=rows,
        in_specs=[VMEM] * 3,
        out_specs=VMEM,
        compiler_params=roomy(16),
        name="residual",
    )(sums, hpsi_rows, psi_rows)
    return (from_rows(hpsi, owned), from_rows(residual_rows, owned))


def solution(mesh):
    placed = (
        P(("groups", "renv"), None),
        P("groups", None),
        P(("groups", "renv"), None),
        P(("groups", "renv"), None),
        P(("groups", "renv"), None, None),
        P(("groups", "renv"), None, None),
        P(("groups", "renv"), None, None),
        P(("groups", "renv"), None, None),
        P(("groups", "renv")),
        P(("groups", "renv")),
        P(("groups", "renv")),
    )
    return jax.shard_map(
        shards,
        mesh=mesh,
        in_specs=placed,
        out_specs=(P(("groups", "renv"), None), P(("groups", "renv"), None)),
        check_vma=False,
    )
```

profile of v0, /device:TPU:0, one launch (start us, length us, event | category | flops | bytes accessed | tf_op | source)
XLA Modules:
  0.0 64.0 jit_solution(13566911842327431105)
XLA Ops:
  0.6 2.2 %gather_blocks.1.sent_hbm = f32[16,128,128]{2,1,0:T(8,128)} custom-call(s32[16]{0:T(128)} %bitcast.52, f32[1024,128]{1,0:T(8,128)} %bitcast.35), custom_call_target="tpu_custom_call" | custom-call | tf_op jit(solution)/shard_map/gather_blocks/pallas_call | solution.py:245
  2.8 7.4 %all-to-all-start = ((f32[16,1,128,128]{3,2,1,0:T(8,128)}), f32[16,1,128,128]{3,2,1,0:T(8,128)S(1)}, u32[]{:S(2)}, u32[]{:S(2)}) async-start(f32[16,1,128,128]{3,2,1,0:T(8,128)} %bitcast.47), calls=%async_computation | async-start | bytes 2097152 | tf_op jit(solution)/shard_map/all_to_all | solution.py:254
  10.2 1.2 %index_rows.1 = s32[1,128]{1,0:T(1,128)} custom-call(f32[16,128,128]{2,1,0:T(8,128)} %gather_blocks.1.sent_hbm, s32[1,2,16]{2,1,0:T(2,128)} %bitcast.50, s32[1,2,16]{2,1,0:T(2,128)} %bitcast.51), custom_call_target="tpu_custom_call" | custom-call | flops 1000000 | bytes 65536 | tf_op jit(solution)/shard_map/index_rows/pallas_call | solution.py:258
  11.5 0.4 collective-permute-start
  11.9 1.0 %collective-permute-done = s32[1,128]{1,0:T(1,128)S(1)} collective-permute-done((s32[1,128]{1,0:T(1,128)}, s32[1,128]{1,0:T(1,128)S(1)}, u32[]{:S(2)}, u32[]{:S(2)}) %collective-permute-start) | collective-permute-done | bytes 544 | tf_op jit(solution)/shard_map/ppermute | solution.py:269
  12.9 0.6 pad_add_fusion.2
  13.5 1.8 %collective-permute-start.1 = (s32[2,128]{1,0:T(2,128)S(1)}, s32[2,128]{1,0:T(2,128)S(1)}, u32[]{:S(2)}, u32[]{:S(2)}) collective-permute-start(s32[2,128]{1,0:T(2,128)S(1)} %pad_add_fusion.2), channel_id=1, source_target_pairs={{0,2},{1,3},{2,0},{3,1},{4,6},{5,7},{6,4},{7,5},{8,10},{9,11},{10,... | collective-permute-start | bytes 3080 | tf_op jit(solution)/shard_map/ppermute | solution.py:269
  15.3 3.2 %collective-permute-done.1 = s32[2,128]{1,0:T(2,128)S(1)} collective-permute-done((s32[2,128]{1,0:T(2,128)S(1)}, s32[2,128]{1,0:T(2,128)S(1)}, u32[]{:S(2)}, u32[]{:S(2)}) %collective-permute-start.1) | collective-permute-done | bytes 1056 | tf_op jit(solution)/shard_map/ppermute | solution.py:269
  18.5 0.6 pad_add_fusion.1
  19.1 0.5 collective-permute-start.2
  19.6 8.8 %collective-permute-done.2 = s32[4,128]{1,0:T(4,128)S(1)} collective-permute-done((s32[4,128]{1,0:T(4,128)S(1)}, s32[4,128]{1,0:T(4,128)S(1)}, u32[]{:S(2)}, u32[]{:S(2)}) %collective-permute-start.2) | collective-permute-done | bytes 2080 | tf_op jit(solution)/shard_map/ppermute | solution.py:269
  28.4 0.6 pad_add_fusion
  29.0 4.4 %collective-permute-start.3 = (s32[8,128]{1,0:T(8,128)S(1)}, s32[8,128]{1,0:T(8,128)S(1)}, u32[]{:S(2)}, u32[]{:S(2)}) collective-permute-start(s32[8,128]{1,0:T(8,128)S(1)} %pad_add_fusion), channel_id=1, source_target_pairs={{0,8},{1,9},{2,10},{3,11},{4,12},{5,13},{6,14},{7,15},{8,0},{9,1},... | collective-permute-start | bytes 12296 | tf_op jit(solution)/shard_map/ppermute | solution.py:269
  33.4 5.3 %turn.1 = (bf16[16,128,512]{2,1,0:T(8,128)(2,1)}, bf16[16,128,256]{2,1,0:T(8,128)(2,1)}, bf16[8,128,256]{2,1,0:T(8,128)(2,1)}) custom-call(f32[16,128,128]{2,1,0:T(8,128)} %gather_blocks.1.sent_hbm, s32[1,2,16]{2,1,0:T(2,128)} %bitcast.41, s32[1,2,16]{2,1,0:T(2,128)} %bitcast.43, f32[1024,128]{1,0:T(8,128)} %bitcast.36, f32[2048,128]{1,0:T(8,128)} %bitcast.48), custom_call_target="tpu_custom_call" | custom-call | flops 1000000 | bytes 65536 | tf_op jit(solution)/shard_map/turn/pallas_call | solution.py:272
  38.6 0.0 copy-start.9
  38.6 6.2 %local_terms.1 = (f32[8,128,128]{2,1,0:T(8,128)}, f32[8,128]{1,0:T(8,128)}) custom-call(s32[32]{0:T(128)} %block_ref.1, s32[32]{0:T(128)} %left_ref.1, s32[32]{0:T(128)} %right_ref.1, f32[1024,128]{1,0:T(8,128)} %bitcast.37, f32[8192,128]{1,0:T(8,128)} %bitcast.45, bf16[8,128,256]{2,1,0:T(8,128)(2,1)} %get-tuple-element.11.psis_ref, ...), custom_call_target="tpu_custom_call" | custom-call | flops 1000000 | bytes 65536 | tf_op jit(solution)/shard_map/local_terms/pallas_call | solution.py:287
  44.8 0.0 collective-permute-done.3
  44.8 0.0 copy-done.9
  44.9 0.0 copy-start.1
  44.9 1.6 %copy-done.1 = bf16[16,128,512]{2,1,0:T(8,128)(2,1)S(1)} copy-done((bf16[16,128,512]{2,1,0:T(8,128)(2,1)S(1)}, bf16[16,128,512]{2,1,0:T(8,128)(2,1)}, u32[]{:S(2)}) %copy-start.1) | copy-done | bytes 2097176
  46.5 0.0 copy-start.3
  46.5 4.0 %adjoint_blocks.1 = (f32[16,128,128]{2,1,0:T(8,128)S(1)}, bf16[16,256,256]{2,1,0:T(8,128)(2,1)S(1)}) custom-call(s32[1]{0:T(128)} %bitcast.17.refs_0_, s32[16,128]{1,0:T(8,128)S(1)} %concatenate.18.refs_1_, f32[8192,128]{1,0:T(8,128)} %bitcast.46, bf16[16,128,512]{2,1,0:T(8,128)(2,1)S(1)} %copy-done.1), custom_call_target="tpu_custom_call" | custom-call | flops 1000000 | bytes 65536 | tf_op jit(solution)/shard_map/adjoint_blocks/pallas_call | solution.py:298
  50.4 0.0 copy-start.6
  50.4 1.3 %copy-done.6 = bf16[16,256,256]{2,1,0:T(8,128)(2,1)} copy-done((bf16[16,256,256]{2,1,0:T(8,128)(2,1)}, bf16[16,256,256]{2,1,0:T(8,128)(2,1)S(1)}, u32[]{:S(2)}) %copy-start.6) | copy-done | bytes 2097176
  51.8 0.0 copy-start.4
  51.8 0.0 copy-start.5
  51.8 0.0 copy-start.8
  51.8 0.0 all-to-all-done
  51.8 0.0 copy-done.3
  51.8 0.8 %overlap.1 = f32[16,8,128]{2,1,0:T(8,128)} custom-call(f32[16,128,128]{2,1,0:T(8,128)S(1)} %bitcast.39, f32[16,128,128]{2,1,0:T(8,128)S(1)} %get-tuple-element.17.adjoint_ref, f32[8,128]{1,0:T(8,128)S(1)} %copy-done.3), custom_call_target="tpu_custom_call" | custom-call | tf_op jit(solution)/shard_map/overlap/pallas_call | solution.py:308
  52.6 3.5 %all-to-all-start.1 = ((f32[16,8,128]{2,1,0:T(8,128)}), f32[16,8,128]{2,1,0:T(8,128)S(1)}, u32[]{:S(2)}, u32[]{:S(2)}) async-start(f32[16,8,128]{2,1,0:T(8,128)} %overlap.1), calls=%async_computation.1 | async-start | bytes 131072 | tf_op jit(solution)/shard_map/all_to_all | solution.py:316
  56.1 0.0 copy-done.4
  56.1 0.0 copy-done.5
  56.1 0.0 copy-done.8
  56.1 0.0 copy-start.2
  56.1 1.2 %copy-done.2 = bf16[16,128,256]{2,1,0:T(8,128)(2,1)S(1)} copy-done((bf16[16,128,256]{2,1,0:T(8,128)(2,1)S(1)}, bf16[16,128,256]{2,1,0:T(8,128)(2,1)}, u32[]{:S(2)}) %copy-start.2) | copy-done | bytes 1048600
  57.4 0.0 copy-start.7
  57.4 1.6 %copy-done.7 = bf16[16,256,256]{2,1,0:T(8,128)(2,1)S(1)} copy-done((bf16[16,256,256]{2,1,0:T(8,128)(2,1)S(1)}, bf16[16,256,256]{2,1,0:T(8,128)(2,1)}, u32[]{:S(2)}) %copy-start.7) | copy-done | bytes 2097176
  59.0 0.0 copy-start
  59.0 4.0 %remote_terms.1 = (f32[1024,128]{1,0:T(8,128)S(1)}, f32[1024,128]{1,0:T(8,128)}) custom-call(s32[1,2,16]{2,1,0:T(2,128)S(1)} %bitcast.42, s32[1,2,16]{2,1,0:T(2,128)S(1)} %bitcast.44, f32[16,128,128]{2,1,0:T(8,128)S(1)} %bitcast.40, f32[8,128,128]{2,1,0:T(8,128)S(1)} %copy-done.8, bf16[16,256,256]{2,1,0:T(8,128)(2,1)S(1)} %copy-done.7, ...), custom_call_target="tpu_custom_call" | custom-call | flops 4000000000 | bytes 6291456 | tf_op jit(solution)/shard_map/remote_terms/pallas_call | solution.py:318
  63.0 0.0 all-to-all-done.1.sums_ref
  63.0 0.0 copy-done
  63.0 1.0 %residual.1 = f32[1024,128]{1,0:T(8,128)} custom-call(f32[16,8,128]{2,1,0:T(8,128)S(1)} %all-to-all-done.1.sums_ref, f32[1024,128]{1,0:T(8,128)S(1)} %get-tuple-element.19.hpsi_rows, f32[1024,128]{1,0:T(8,128)S(1)} %bitcast.38), custom_call_target="tpu_custom_call" | custom-call | tf_op jit(solution)/shard_map/residual/pallas_call | solution.py:333
  (1 shorter events, 0.0 us)
Async XLA Ops:
  2.8 48.9 %all-to-all-start = ((f32[16,1,128,128]{3,2,1,0:T(8,128)}), f32[16,1,128,128]{3,2,1,0:T(8,128)S(1)}, u32[]{:S(2)}, u32[]{:S(2)}) async-start(f32[16,1,128,128]{3,2,1,0:T(8,128)} %bitcast.47), calls=%async_computation | async-start | bytes 2097152 | tf_op jit(solution)/shard_map/all_to_all | solution.py:254
  11.5 1.4 %collective-permute-start = (s32[1,128]{1,0:T(1,128)}, s32[1,128]{1,0:T(1,128)S(1)}, u32[]{:S(2)}, u32[]{:S(2)}) collective-permute-start(s32[1,128]{1,0:T(1,128)} %index_rows.1), channel_id=1, source_target_pairs={{0,1},{1,0},{2,3},{3,2},{4,5},{5,4},{6,7},{7,6},{8,9},{9,8},{10,11... | collective-permute-start | bytes 1544 | tf_op jit(solution)/shard_map/ppermute | solution.py:269
  13.5 5.0 %collective-permute-start.1 = (s32[2,128]{1,0:T(2,128)S(1)}, s32[2,128]{1,0:T(2,128)S(1)}, u32[]{:S(2)}, u32[]{:S(2)}) collective-permute-start(s32[2,128]{1,0:T(2,128)S(1)} %pad_add_fusion.2), channel_id=1, source_target_pairs={{0,2},{1,3},{2,0},{3,1},{4,6},{5,7},{6,4},{7,5},{8,10},{9,11},{10,... | collective-permute-start | bytes 3080 | tf_op jit(solution)/shard_map/ppermute | solution.py:269
  19.1 9.2 %collective-permute-start.2 = (s32[4,128]{1,0:T(4,128)S(1)}, s32[4,128]{1,0:T(4,128)S(1)}, u32[]{:S(2)}, u32[]{:S(2)}) collective-permute-start(s32[4,128]{1,0:T(4,128)S(1)} %pad_add_fusion.1), channel_id=1, source_target_pairs={{0,4},{1,5},{2,6},{3,7},{4,0},{5,1},{6,2},{7,3},{8,12},{9,13},{10,... | collective-permute-start | bytes 6152 | tf_op jit(solution)/shard_map/ppermute | solution.py:269
  29.0 15.8 %collective-permute-start.3 = (s32[8,128]{1,0:T(8,128)S(1)}, s32[8,128]{1,0:T(8,128)S(1)}, u32[]{:S(2)}, u32[]{:S(2)}) collective-permute-start(s32[8,128]{1,0:T(8,128)S(1)} %pad_add_fusion), channel_id=1, source_target_pairs={{0,8},{1,9},{2,10},{3,11},{4,12},{5,13},{6,14},{7,15},{8,0},{9,1},... | collective-permute-start | bytes 12296 | tf_op jit(solution)/shard_map/ppermute | solution.py:269
  38.6 6.2 %copy-start.9 = (s32[1,128]{1,0:T(1,128)S(1)}, s32[1,128]{1,0:T(1,128)}, u32[]{:S(2)}) copy-start(s32[1,128]{1,0:T(1,128)} %index_rows.1) | copy-start | bytes 1540
  44.9 1.6 %copy-start.1 = (bf16[16,128,512]{2,1,0:T(8,128)(2,1)S(1)}, bf16[16,128,512]{2,1,0:T(8,128)(2,1)}, u32[]{:S(2)}) copy-start(bf16[16,128,512]{2,1,0:T(8,128)(2,1)} %get-tuple-element.14.refs_3_) | copy-start | bytes 6291460
  46.5 5.3 %copy-start.3 = (f32[8,128]{1,0:T(8,128)S(1)}, f32[8,128]{1,0:T(8,128)}, u32[]{:S(2)}) copy-start(f32[8,128]{1,0:T(8,128)} %get-tuple-element.18.near_sums_ref) | copy-start | bytes 12292
  50.4 1.3 %copy-start.6 = (bf16[16,256,256]{2,1,0:T(8,128)(2,1)}, bf16[16,256,256]{2,1,0:T(8,128)(2,1)S(1)}, u32[]{:S(2)}) copy-start(bf16[16,256,256]{2,1,0:T(8,128)(2,1)S(1)} %get-tuple-element.15.lefts_ref) | copy-start | bytes 6291460
  51.8 4.3 %copy-start.4 = (s32[16,1,2]{0,2,1:T(2,128)S(1)}, s32[16,1,2]{0,2,1:T(2,128)}, u32[]{:S(2)}) copy-start(s32[16,1,2]{0,2,1:T(2,128)} %param.17) | copy-start | bytes 388
  51.8 4.4 %copy-start.5 = (s32[16,1,2]{0,2,1:T(2,128)S(1)}, s32[16,1,2]{0,2,1:T(2,128)}, u32[]{:S(2)}) copy-start(s32[16,1,2]{0,2,1:T(2,128)} %param.18) | copy-start | bytes 388
  51.8 4.4 %copy-start.8 = (f32[8,128,128]{2,1,0:T(8,128)S(1)}, f32[8,128,128]{2,1,0:T(8,128)}, u32[]{:S(2)}) copy-start(f32[8,128,128]{2,1,0:T(8,128)} %get-tuple-element.13.near_ref) | copy-start | bytes 1572868
  52.6 10.4 %all-to-all-start.1 = ((f32[16,8,128]{2,1,0:T(8,128)}), f32[16,8,128]{2,1,0:T(8,128)S(1)}, u32[]{:S(2)}, u32[]{:S(2)}) async-start(f32[16,8,128]{2,1,0:T(8,128)} %overlap.1), calls=%async_computation.1 | async-start | bytes 131072 | tf_op jit(solution)/shard_map/all_to_all | solution.py:316
  56.1 1.2 %copy-start.2 = (bf16[16,128,256]{2,1,0:T(8,128)(2,1)S(1)}, bf16[16,128,256]{2,1,0:T(8,128)(2,1)}, u32[]{:S(2)}) copy-start(bf16[16,128,256]{2,1,0:T(8,128)(2,1)} %get-tuple-element.12.rights_ref) | copy-start | bytes 3145732
  57.4 1.6 %copy-start.7 = (bf16[16,256,256]{2,1,0:T(8,128)(2,1)S(1)}, bf16[16,256,256]{2,1,0:T(8,128)(2,1)}, u32[]{:S(2)}) copy-start(bf16[16,256,256]{2,1,0:T(8,128)(2,1)} %copy-done.6) | copy-start | bytes 6291460
  59.0 4.1 %copy-start = (f32[8,16384]{1,0:T(8,128)S(1)}, f32[8,16384]{1,0:T(8,128)}, u32[]{:S(2)}) copy-start(f32[8,16384]{1,0:T(8,128)} %param.11) | copy-start | bytes 1572868
where the time goes:
time: 64.5 us; the launch traced here: 64 us
  Pallas kernels  24.8 us (38%)
  starting transfers between devices  17.9 us (28%)
  waiting for transfers between devices  13 us (20%)
  local copies, waits for them, and re-layouts  5.77 us (9%)
  other arithmetic  1.82 us (3%)
  between operations  0.75 us (1%)
    ppermute x4, waiting for transfers between devices, shards(): lax.ppermute(meta, 'renv', [(s, s ^ step) for s in range(peers)])  13 us
    all_to_all x1, starting transfers between devices, shards(): lax.all_to_all(sent.reshape(peers, slots, sector, sector), 'renv', split_...  7.37 us
    ppermute x4, starting transfers between devices, shards(): lax.ppermute(meta, 'renv', [(s, s ^ step) for s in range(peers)])  7.06 us
    pallas_call x1, Pallas kernels, shards(): pl.pallas_call(local_kernel, out_shape=(mats, tile), in_specs=[SMEM] * 3...  6.21 us
    unnamed x20, local copies, waits for them, and re-layouts  5.74 us
    pallas_call x1, Pallas kernels, shards(): pl.pallas_call(turn_kernel, out_shape=(jax.ShapeDtypeStruct((count, secto...  5.27 us
    pallas_call x1, Pallas kernels, shards(): pl.pallas_call(remote_kernel, out_shape=(rows, rows), in_specs=[SMEM] * 2...  4.04 us
    pallas_call x1, Pallas kernels, shards(): pl.pallas_call(lambda *refs: adjoint_kernel(slots, terms, *refs), out_sha...  3.96 us
  transfers between devices with their start and end apart: 6, of which 3 were waited for; matrix products, arithmetic and copies ran while one was open for 3% of the time, Pallas kernels for 32%

commit v1 on v0

--- a/solution.py
+++ b/solution.py
@@ -73,27 +73,25 @@
     return pltpu.CompilerParams(vmem_limit_bytes=mib * MIB)
 
 
-def gather_kernel(block_ref, psi_rows, out_hbm, stage, sems):
+def gather_kernel(me_ref, block_ref, left_ref, live_ref, psi_rows, out_hbm, table_ref, stage, sems):
+    slots, terms, _ = left_ref.shape
     puts = []
     for i in range(stage.shape[0]):
         stage[i] = pick(psi_rows, block_ref[i])
         put = pltpu.make_async_copy(stage.at[i], out_hbm.at[i], sems.at[i])
         put.start()
         puts.append(put)
-    for put in puts:
-        put.wait()
-
-
-def index_kernel(sent_hbm, left_ref, live_ref, meta_ref):
-    slots, terms, peers = left_ref.shape
-    lane = lax.broadcasted_iota(jnp.int32, meta_ref.shape, 1)
-    values = jnp.zeros(meta_ref.shape, jnp.int32)
-    for i in range(peers * slots):
+    table_ref[...] = jnp.zeros(table_ref.shape, table_ref.dtype)
+    lane = lax.broadcasted_iota(jnp.int32, (1, table_ref.shape[1]), 1)
+    values = jnp.zeros(lane.shape, jnp.int32)
+    for i in range(stage.shape[0]):
         for g in range(terms):
             at = i * 2 * terms + g
             values = jnp.where(lane == at, left_ref[i % slots, g, i // slots], values)
             values = jnp.where(lane == at + terms, live_ref[i % slots, g, i // slots], values)
-    meta_ref[...] = values
+    table_ref[pl.ds(me_ref[0], 1), :] = values
+    for put in puts:
+        put.wait()
 
 
 def turn_kernel(sent_hbm, rindex_ref, out_index_ref, psi_rows, right_rows, turned_ref, rights_ref, psis_ref, stacks_ref):
@@ -154,7 +152,7 @@
 
     def sender(i, carry):
         weights = []
-        row = lax.bitwise_xor(i // slots, me_ref[0])
+        row = i // slots
         base = (me_ref[0] * slots + i % slots) * 2 * terms
         for g in range(terms):
             live = meta_ref[row, base + terms + g].astype(F32)
@@ -242,32 +240,20 @@
     mats = jax.ShapeDtypeStruct((owned, sector, sector), F32)
     tile = jax.ShapeDtypeStruct((SUB, sector), F32)
 
-    sent = pl.pallas_call(
+    lanes = -(-count * 2 * terms // 128) * 128
+    table = jax.ShapeDtypeStruct((-(-peers // 128) * 128, lanes), jnp.int32)
+    sent, meta = pl.pallas_call(
         gather_kernel,
-        out_shape=blocks,
-        in_specs=[SMEM, VMEM],
-        out_specs=HBM,
+        out_shape=(blocks, table),
+        in_specs=[SMEM] * 4 + [VMEM],
+        out_specs=(HBM, VMEM),
         scratch_shapes=[pltpu.VMEM(blocks.shape, F32), pltpu.SemaphoreType.DMA((count,))],
         compiler_params=roomy(56),
         name="gather_blocks",
-    )(send_block.reshape(-1), psi_rows)
+    )(me, send_block.reshape(-1), *by_slot[:2], psi_rows)
+    meta = lax.psum(meta, "renv")
     came = lax.all_to_all(sent.reshape(peers, slots, sector, sector), "renv", split_axis=0, concat_axis=0, tiled=True)
     came = came.reshape(count, sector, sector)
-
-    lanes = -(-count * 2 * terms // 128) * 128
-    meta = pl.pallas_call(
-        index_kernel,
-        out_shape=jax.ShapeDtypeStruct((1, lanes), jnp.int32),
-        in_specs=[HBM] + [SMEM] * 2,
-        out_specs=VMEM,
-        compiler_params=roomy(56),
-        cost_estimate=LIGHT,
-        name="index_rows",
-    )(sent, *by_slot[:2])
-    step = 1
-    while step < peers:
-        meta = jnp.concatenate([meta, lax.ppermute(meta, "renv", [(s, s ^ step) for s in range(peers)])], axis=0)
-        step *= 2
 
     turned, right_parts, psi_parts = pl.pallas_call(
         turn_kernel,

time: 64.5 us -> 142 us (2.20)
  waiting for transfers between devices: 13 us -> 83.1 us
  between operations: 0.75 us -> 14.1 us
  starting transfers between devices: 17.9 us -> 13.7 us
  other arithmetic: 1.82 us -> 0 us
    psum x0 -> x1, waiting for transfers between devices: none -> 82.4 us  [shards(): meta = lax.psum(meta, 'renv')]
    ppermute x4 -> x0, waiting for transfers between devices: 13 us -> none  [shards(): lax.ppermute(meta, 'renv', [(s, s ^ step) for s in range(peers)])]
    ppermute x4 -> x0, starting transfers between devices: 7.06 us -> none  [shards(): lax.ppermute(meta, 'renv', [(s, s ^ step) for s in range(peers)])]
    all_to_all x1, starting transfers between devices: 3.5 us -> 6.3 us  [shards(): sums = lax.all_to_all(sums, 'renv', split_axis=0, concat_axis=0, tiled=True)]
    concatenate x3 -> x0, other arithmetic: 1.82 us -> none  [shards(): jnp.concatenate([meta, lax.ppermute(meta, 'renv', [(s, s ^ step) for s in...]
    pallas_call x2 -> x1, Pallas kernels: 3.45 us -> 2.81 us  [shards(): pl.pallas_call(gather_kernel, out_shape=(blocks, table), in_specs=[SMEM]...]
  transfers between devices with their start and end apart: 6 -> 3, of which waited for: 3 -> 1; matrix products, arithmetic and copies ran while one was open for 3% -> 0% of each run, Pallas kernels for 32% -> 14%
where the time goes in v1:
time: 142 us
  waiting for transfers between devices  83.1 us (59%)
  Pallas kernels  24.1 us (17%)
  between operations  14.1 us (10%)
  starting transfers between devices  13.7 us (10%)
  local copies, waits for them, and re-layouts  6.59 us (5%)
    psum x1, waiting for transfers between devices, shards(): meta = lax.psum(meta, 'renv')  82.4 us
    all_to_all x1, starting transfers between devices, shards(): lax.all_to_all(sent.reshape(peers, slots, sector, sector), 'renv', split_...  7.37 us
    unnamed x20, local copies, waits for them, and re-layouts  6.59 us
    all_to_all x1, starting transfers between devices, shards(): sums = lax.all_to_all(sums, 'renv', split_axis=0, concat_axis=0, tiled=True)  6.3 us
    pallas_call x1, Pallas kernels, shards(): pl.pallas_call(local_kernel, out_shape=(mats, tile), in_specs=[SMEM] * 3...  6.23 us
    pallas_call x1, Pallas kernels, shards(): pl.pallas_call(turn_kernel, out_shape=(jax.ShapeDtypeStruct((count, secto...  5.28 us
    pallas_call x1, Pallas kernels, shards(): pl.pallas_call(remote_kernel, out_shape=(rows, rows), in_specs=[SMEM] * 2...  4.04 us
    pallas_call x1, Pallas kernels, shards(): pl.pallas_call(lambda *refs: adjoint_kernel(slots, terms, *refs), out_sha...  3.94 us
  transfers between devices with their start and end apart: 3, of which 1 were waited for; matrix products, arithmetic and copies ran while one was open for 0% of the time, Pallas kernels for 14%

profile of v1, /device:TPU:0, one launch (start us, length us, event | category | flops | bytes accessed | tf_op | source)
XLA Modules:
  0.0 141.7 jit_solution(3085694949194555787)
XLA Ops:
  7.2 2.8 %gather_blocks.1 = (f32[16,128,128]{2,1,0:T(8,128)}, s32[128,128]{1,0:T(8,128)}) custom-call(s32[1]{0:T(128)} %bitcast.2.me_ref.refs_0_, s32[16]{0:T(128)} %bitcast.52, s32[1,2,16]{2,1,0:T(2,128)} %bitcast.50, s32[1,2,16]{2,1,0:T(2,128)} %bitcast.51, f32[1024,128]{1,0:T(8,128)} %bitcast.35), custom_call_target="tpu_custom_call" | custom-call | tf_op jit(solution)/shard_map/gather_blocks/pallas_call | solution.py:245
  10.0 7.4 %all-to-all-start = ((f32[16,1,128,128]{3,2,1,0:T(8,128)}), f32[16,1,128,128]{3,2,1,0:T(8,128)S(1)}, u32[]{:S(2)}, u32[]{:S(2)}) async-start(f32[16,1,128,128]{3,2,1,0:T(8,128)} %bitcast.47), calls=%async_computation | async-start | bytes 2097152 | tf_op jit(solution)/shard_map/all_to_all | solution.py:255
  17.4 0.0 all-reduce.2.cloned.1.call-start
  17.4 0.7 all-reduce.2.cloned.1.call-update
  18.1 5.3 %turn.1 = (bf16[16,128,512]{2,1,0:T(8,128)(2,1)}, bf16[16,128,256]{2,1,0:T(8,128)(2,1)}, bf16[8,128,256]{2,1,0:T(8,128)(2,1)}) custom-call(f32[16,128,128]{2,1,0:T(8,128)} %get-tuple-element.13.sent_hbm, s32[1,2,16]{2,1,0:T(2,128)} %bitcast.41, s32[1,2,16]{2,1,0:T(2,128)} %bitcast.43, f32[1024,128]{1,0:T(8,128)} %bitcast.36, f32[2048,128]{1,0:T(8,128)} %bitcast.48), custom_call_target="tpu_custom_call" | custom-call | flops 1000000 | bytes 65536 | tf_op jit(solution)/shard_map/turn/pallas_call | solution.py:258
  23.4 6.2 %local_terms.1 = (f32[8,128,128]{2,1,0:T(8,128)}, f32[8,128]{1,0:T(8,128)}) custom-call(s32[32]{0:T(128)} %block_ref.1, s32[32]{0:T(128)} %left_ref.1, s32[32]{0:T(128)} %right_ref.1, f32[1024,128]{1,0:T(8,128)} %bitcast.37, f32[8192,128]{1,0:T(8,128)} %bitcast.45, bf16[8,128,256]{2,1,0:T(8,128)(2,1)} %get-tuple-element.14.psis_ref, ...), custom_call_target="tpu_custom_call" | custom-call | flops 1000000 | bytes 65536 | tf_op jit(solution)/shard_map/local_terms/pallas_call | solution.py:273
  29.6 82.4 %all-reduce.2.cloned.1.call-done.refs_1_ = s32[128,128]{1,0:T(8,128)} async-done(((s32[128,128]{1,0:T(8,128)}), s32[128,128]{1,0:T(8,128)}) %all-reduce.2.cloned.1.call-update) | async-done | bytes 65552 | tf_op jit(solution)/shard_map/psum | solution.py:254
  112.0 0.0 copy-start.1
  112.0 1.6 %copy-done.1 = bf16[16,128,512]{2,1,0:T(8,128)(2,1)S(1)} copy-done((bf16[16,128,512]{2,1,0:T(8,128)(2,1)S(1)}, bf16[16,128,512]{2,1,0:T(8,128)(2,1)}, u32[]{:S(2)}) %copy-start.1) | copy-done | bytes 2097176
  113.6 0.0 copy-start.3
  113.6 0.8 copy-done.3
  114.5 0.0 copy-start.4
  114.5 3.9 %adjoint_blocks.1 = (f32[16,128,128]{2,1,0:T(8,128)S(1)}, bf16[16,256,256]{2,1,0:T(8,128)(2,1)S(1)}) custom-call(s32[1]{0:T(128)} %bitcast.2.me_ref.refs_0_, s32[128,128]{1,0:T(8,128)S(1)} %copy-done.3, f32[8192,128]{1,0:T(8,128)} %bitcast.46, bf16[16,128,512]{2,1,0:T(8,128)(2,1)S(1)} %copy-done.1), custom_call_target="tpu_custom_call" | custom-call | flops 1000000 | bytes 65536 | tf_op jit(solution)/shard_map/adjoint_blocks/pallas_call | solution.py:284
  118.4 0.0 copy-start.7
  118.4 1.3 copy-done.7
  119.8 0.0 copy-start.5
  119.8 0.0 copy-start.6
  119.8 0.0 copy-start.9
  119.8 0.0 all-to-all-done
  119.8 0.0 copy-done.4
  119.8 0.8 overlap.1
  120.6 6.3 %all-to-all-start.1 = ((f32[16,8,128]{2,1,0:T(8,128)}), f32[16,8,128]{2,1,0:T(8,128)S(1)}, u32[]{:S(2)}, u32[]{:S(2)}) async-start(f32[16,8,128]{2,1,0:T(8,128)} %overlap.1), calls=%async_computation.1 | async-start | bytes 131072 | tf_op jit(solution)/shard_map/all_to_all | solution.py:302
  126.9 0.0 copy-done.5
  126.9 0.0 copy-done.6
  126.9 0.0 copy-done.9
  126.9 0.0 copy-start.2
  126.9 1.2 copy-done.2
  128.2 0.0 copy-start.8
  128.2 1.6 %copy-done.8 = bf16[16,256,256]{2,1,0:T(8,128)(2,1)S(1)} copy-done((bf16[16,256,256]{2,1,0:T(8,128)(2,1)S(1)}, bf16[16,256,256]{2,1,0:T(8,128)(2,1)}, u32[]{:S(2)}) %copy-start.8) | copy-done | bytes 2097176
  129.7 0.0 copy-start
  129.7 4.0 %remote_terms.1 = (f32[1024,128]{1,0:T(8,128)S(1)}, f32[1024,128]{1,0:T(8,128)}) custom-call(s32[1,2,16]{2,1,0:T(2,128)S(1)} %bitcast.42, s32[1,2,16]{2,1,0:T(2,128)S(1)} %bitcast.44, f32[16,128,128]{2,1,0:T(8,128)S(1)} %bitcast.40, f32[8,128,128]{2,1,0:T(8,128)S(1)} %copy-done.9, bf16[16,256,256]{2,1,0:T(8,128)(2,1)S(1)} %copy-done.8, ...), custom_call_target="tpu_custom_call" | custom-call | flops 4000000000 | bytes 6291456 | tf_op jit(solution)/shard_map/remote_terms/pallas_call | solution.py:304
  133.8 0.0 all-to-all-done.1.sums_ref
  133.8 0.0 copy-done
  133.8 1.0 residual.1
Async XLA Ops:
  10.0 109.8 %all-to-all-start = ((f32[16,1,128,128]{3,2,1,0:T(8,128)}), f32[16,1,128,128]{3,2,1,0:T(8,128)S(1)}, u32[]{:S(2)}, u32[]{:S(2)}) async-start(f32[16,1,128,128]{3,2,1,0:T(8,128)} %bitcast.47), calls=%async_computation | async-start | bytes 2097152 | tf_op jit(solution)/shard_map/all_to_all | solution.py:255
  17.4 94.7 %all-reduce.2.cloned.1.call-start = ((), (), s32[]{:S(2)}) async-start(), calls=%async_computation.2 | async-start | bytes 131072 | tf_op jit(solution)/shard_map/psum | solution.py:254
  112.0 1.6 %copy-start.1 = (bf16[16,128,512]{2,1,0:T(8,128)(2,1)S(1)}, bf16[16,128,512]{2,1,0:T(8,128)(2,1)}, u32[]{:S(2)}) copy-start(bf16[16,128,512]{2,1,0:T(8,128)(2,1)} %get-tuple-element.18.refs_3_) | copy-start | bytes 6291460
  113.6 0.8 copy-start.3
  114.5 5.3 %copy-start.4 = (f32[8,128]{1,0:T(8,128)S(1)}, f32[8,128]{1,0:T(8,128)}, u32[]{:S(2)}) copy-start(f32[8,128]{1,0:T(8,128)} %get-tuple-element.22.near_sums_ref) | copy-start | bytes 12292
  118.4 1.3 copy-start.7
  119.8 7.1 %copy-start.5 = (s32[16,1,2]{0,2,1:T(2,128)S(1)}, s32[16,1,2]{0,2,1:T(2,128)}, u32[]{:S(2)}) copy-start(s32[16,1,2]{0,2,1:T(2,128)} %param.17) | copy-start | bytes 388
  119.8 7.2 %copy-start.6 = (s32[16,1,2]{0,2,1:T(2,128)S(1)}, s32[16,1,2]{0,2,1:T(2,128)}, u32[]{:S(2)}) copy-start(s32[16,1,2]{0,2,1:T(2,128)} %param.18) | copy-start | bytes 388
  119.8 7.2 %copy-start.9 = (f32[8,128,128]{2,1,0:T(8,128)S(1)}, f32[8,128,128]{2,1,0:T(8,128)}, u32[]{:S(2)}) copy-start(f32[8,128,128]{2,1,0:T(8,128)} %get-tuple-element.16.near_ref) | copy-start | bytes 1572868
  120.6 13.2 %all-to-all-start.1 = ((f32[16,8,128]{2,1,0:T(8,128)}), f32[16,8,128]{2,1,0:T(8,128)S(1)}, u32[]{:S(2)}, u32[]{:S(2)}) async-start(f32[16,8,128]{2,1,0:T(8,128)} %overlap.1), calls=%async_computation.1 | async-start | bytes 131072 | tf_op jit(solution)/shard_map/all_to_all | solution.py:302
  126.9 1.2 copy-start.2
  128.2 1.6 %copy-start.8 = (bf16[16,256,256]{2,1,0:T(8,128)(2,1)S(1)}, bf16[16,256,256]{2,1,0:T(8,128)(2,1)}, u32[]{:S(2)}) copy-start(bf16[16,256,256]{2,1,0:T(8,128)(2,1)} %copy-done.7) | copy-start | bytes 6291460
  129.7 4.1 %copy-start = (f32[8,16384]{1,0:T(8,128)S(1)}, f32[8,16384]{1,0:T(8,128)}, u32[]{:S(2)}) copy-start(f32[8,16384]{1,0:T(8,128)} %param.11) | copy-start | bytes 1572868
Sparse Core Ops, SparseCore 0:
  21.7 90.3 all-reduce.1
